TPU v7x, 256 devices: a whole 4x4x8 slice. The times are simulated.
256 devices in a mesh: fsdp: 32 (over z_lo, y, x), tok: 8 (over z_hi, core).
Axes of the slice: x: 4, y: 4, z: 8 (z_hi: 4, z_lo: 2; z = z_hi * 2 + z_lo), core: 2. Of those that a mesh axis runs over, the one named last changes fastest.
Arguments:
- tokens: bfloat16 [1024, 8192], P(None, 'tok'), may hold values from -6 to 6
- gate_a: bfloat16 [14336, 8192], P('fsdp', 'tok'), may hold values from -0.0625 to 0.0625
- up_a: bfloat16 [14336, 8192], P('fsdp', 'tok'), may hold values from -0.0625 to 0.0625
- gate_b: bfloat16 [14336, 8192], P('fsdp', 'tok'), may hold values from -0.0625 to 0.0625
- up_b: bfloat16 [14336, 8192], P('fsdp', 'tok'), may hold values from -0.0625 to 0.0625
- matching: int32 [14336], replicated, may hold values from 0 to 14335, as said below
- mixing: float32 [14336], P('fsdp'), may hold values from 0.2 to 0.8
Outputs:
- correlation: bfloat16 [14336, 14336], P('fsdp', 'tok')
- merged_gate: bfloat16 [14336, 8192], P('fsdp', 'tok')
- merged_up: bfloat16 [14336, 8192], P('fsdp', 'tok')
Inputs may be any that keep to these rules, and one draw needn't show every extreme that they name: A permutation of the 14336 units, found in an earlier round by an assignment limited in capacity, so that every block of 448 consecutive positions holds exactly 14 entries from each block of 448 consecutive values. The correlation computed here feeds the next round's matching.
All inputs are finite; a program needn't handle non-finite values.
Results may differ from a plain program's by a relative error of at most 0.0057.
Values may be sent and summed in bfloat16 or wider, within the bound.
A program may use at most 128 MiB of HBM per device.

v0:
```python
import math

import jax
import jax.numpy as jnp
from jax import lax
from jax.sharding import PartitionSpec as P


def blend_rows(own_rows, other_rows, mixing):
    weight = mixing[:, None]
    mixed = (1.0 - weight) * own_rows.astype(jnp.float32) + weight * other_rows.astype(jnp.float32)
    return mixed.astype(jnp.bfloat16)


def body(tokens, gate_a, up_a, gate_b, up_b, matching, mixing):
    fsdp_count = lax.axis_size("fsdp")
    unit_rows = gate_a.shape[0]
    contract = (((1,), (1,)), ((), ()))
    stacked = jnp.concatenate((gate_a, up_a, gate_b, up_b), 0)
    preacts = lax.psum_scatter(
        lax.dot_general(tokens, stacked, contract, preferred_element_type=jnp.float32),
        "tok",
        scatter_dimension=0,
        tiled=True,
    )
    act_a = (jax.nn.silu(preacts[:, :unit_rows]) * preacts[:, unit_rows : 2 * unit_rows]).astype(
        jnp.bfloat16
    )
    act_b = (
        jax.nn.silu(preacts[:, 2 * unit_rows : 3 * unit_rows]) * preacts[:, 3 * unit_rows :]
    ).astype(jnp.bfloat16)
    wide = lax.all_gather(act_b, "fsdp", axis=1, tiled=True)
    rows_a = lax.all_gather(act_a, "tok", axis=0, tiled=True)
    rows_b = lax.all_to_all(wide, "tok", split_axis=1, concat_axis=0, tiled=True)
    summed = lax.dot_general(
        rows_a, rows_b, (((0,), (0,)), ((), ())), preferred_element_type=jnp.float32
    )
    correlation = (summed / math.sqrt(rows_a.shape[0])).astype(jnp.bfloat16)
    capacity = unit_rows // fsdp_count
    own_block = lax.axis_index("fsdp")
    table = matching.reshape(fsdp_count, unit_rows)
    chosen = (table // unit_rows == own_block).astype(jnp.int32)
    slot = jnp.cumsum(chosen, axis=1) - 1
    hits = chosen[:, :, None] * (slot[:, :, None] == jnp.arange(capacity)[None, None, :]).astype(
        jnp.int32
    )
    send_rows = jnp.sum(hits * (table % unit_rows)[:, :, None], axis=1).reshape(-1)
    outgoing_gate = jnp.take(gate_b, send_rows, axis=0).reshape(fsdp_count, capacity, -1)
    outgoing_up = jnp.take(up_b, send_rows, axis=0).reshape(fsdp_count, capacity, -1)
    incoming_gate, incoming_up = (
        lax.all_to_all(outgoing_gate, "fsdp", split_axis=0, concat_axis=0, tiled=True),
        lax.all_to_all(outgoing_up, "fsdp", split_axis=0, concat_axis=0, tiled=True),
    )
    wanted = lax.dynamic_slice_in_dim(matching, own_block * unit_rows, unit_rows, 0)
    anchor = wanted // unit_rows
    match_table = (anchor[:, None] == jnp.arange(fsdp_count)[None, :]).astype(jnp.int32)
    rank = jnp.sum(match_table * (jnp.cumsum(match_table, axis=0) - 1), axis=1)
    position = anchor * capacity + rank
    got_gate = jnp.take(incoming_gate.reshape(fsdp_count * capacity, -1), position, axis=0)
    got_up = jnp.take(incoming_up.reshape(fsdp_count * capacity, -1), position, axis=0)
    merged_gate = blend_rows(gate_a, got_gate, mixing)
    merged_up = blend_rows(up_a, got_up, mixing)
    return (correlation, merged_gate, merged_up)


def solution(mesh):
    placed = (
        P(None, "tok"),
        P("fsdp", "tok"),
        P("fsdp", "tok"),
        P("fsdp", "tok"),
        P("fsdp", "tok"),
        P(),
        P("fsdp"),
    )
    return jax.shard_map(
        body,
        mesh=mesh,
        in_specs=placed,
        out_specs=(P("fsdp", "tok"), P("fsdp", "tok"), P("fsdp", "tok")),
        check_vma=False,
    )
```

profile of v0, /device:TPU:56, one launch (start us, length us, event | category | flops | bytes accessed | tf_op | source)
XLA Modules:
  0.0 392.2 jit_solution(3476818929076838573)
XLA Ops:
  7.2 0.0 copy-start
  7.2 0.0 reduce-scatter.2.cloned.1.call-start
  7.2 1.5 copy-done
  8.8 9.0 %convolution_bitcast_fusion = f32[1024,1792]{0,1:T(8,128)} fusion(bf16[1024,1024]{1,0:T(8,128)(2,1)S(1)} %copy-done, bf16[448,1024]{1,0:T(8,128)(2,1)} %param.13, bf16[448,1024]{1,0:T(8,128)(2,1)} %param.12, bf16[448,1024]{1,0:T(8,128)(2,1)} %param.11, bf16[448,1024]{1,0:T(8,128)(2,1)} %param.10), kind=kOutput, calls=%fused_computation.4 | convolution fusion | flops 3772776448 | bytes 13107200 | tf_op jit(solution)/shard_map/dot_general | solution.py:21
  17.8 0.0 copy-start.4
  17.8 0.0 copy-start.1
  17.8 0.0 reduce-scatter.2.cloned.1.call-update
  17.8 0.0 all-gather.2.cloned.1.call-start
  17.8 85.4 %reduce-scatter.2.cloned.1.call-done = f32[128,1792]{0,1:T(8,128)} async-done(((f32[1024,1792]{0,1:T(8,128)}), f32[128,1792]{0,1:T(8,128)}) %reduce-scatter.2.cloned.1.call-update) | async-done | bytes 917520 | tf_op jit(solution)/shard_map/reduce_scatter | solution.py:20
  103.3 2.0 fusion.7
  105.3 0.0 all-gather.2.cloned.1.call-update
  105.3 0.0 copy-done.4
  105.4 0.1 rem.34
  105.5 0.1 div.37
  105.6 0.1 ne.58
  105.7 1.2 reduce-window.14
  106.9 0.2 slice_reduce_fusion
  107.2 0.1 copy_bitcast_fusion
  107.3 0.3 multiply_reduce_fusion
  107.6 0.1 copy.20
  107.7 0.1 reshape.92
  107.8 0.0 copy-done.1
  107.8 2.7 gather_fusion.2
  110.6 0.0 copy-start.3
  110.6 4.8 %gather_fusion = bf16[448,1024]{1,0:T(8,128)(2,1)} fusion(bf16[448,1024]{1,0:T(8,128)(2,1)} %param.12, s32[1024]{0:T(1024)S(1)} %pad_clamp_fusion.1), kind=kCustom, calls=%fused_computation.clone | custom fusion | bytes 1836800 | tf_op jit(solution)/shard_map/jit(_take)/gather | solution.py:48
  115.4 0.0 copy-done.3
  115.4 2.6 broadcast_select_fusion
  118.0 2.2 reshape.97
  120.2 11.4 %all-to-all-start.2 = ((bf16[32,14,1024]{2,1,0:T(8,128)(2,1)}), bf16[32,14,1024]{2,1,0:T(8,128)(2,1)S(1)}, u32[]{:S(2)}, u32[]{:S(2)}) async-start(bf16[32,14,1024]{2,1,0:T(8,128)(2,1)} %reshape.97), calls=%async_computation.3 | async-start | bytes 2097152 | tf_op jit(solution)/shard_map/all_to_all | solution.py:52
  131.6 2.3 reshape.93
  133.9 13.3 %all-to-all-done.2 = bf16[32,14,1024]{2,1,0:T(8,128)(2,1)S(1)} async-done(((bf16[32,14,1024]{2,1,0:T(8,128)(2,1)}), bf16[32,14,1024]{2,1,0:T(8,128)(2,1)S(1)}, u32[]{:S(2)}, u32[]{:S(2)}) %all-to-all-start.2) | async-done | bytes 917536 | tf_op jit(solution)/shard_map/all_to_all | solution.py:52
  147.3 0.0 copy-start.2
  147.3 7.9 %all-to-all-start.1 = ((bf16[32,14,1024]{2,1,0:T(8,128)(2,1)}), bf16[32,14,1024]{2,1,0:T(8,128)(2,1)}, u32[]{:S(2)}, u32[]{:S(2)}) async-start(bf16[32,14,1024]{2,1,0:T(8,128)(2,1)} %reshape.93), calls=%async_computation.2 | async-start | bytes 2097152 | tf_op jit(solution)/shard_map/all_to_all | solution.py:51
  155.2 112.5 %all-gather.2.cloned.1.call-done = bf16[128,14336]{0,1:T(8,128)(2,1)} async-done(((bf16[128,448]{0,1:T(8,128)(2,1)}), bf16[128,14336]{0,1:T(8,128)(2,1)}) %all-gather.2.cloned.1.call-update) | async-done | bytes 3670032 | tf_op jit(solution)/shard_map/all_gather | solution.py:32
  267.7 6.0 %copy.15 = bf16[128,8,1792]{2,0,1:T(8,128)(2,1)} copy(bf16[128,8,1792]{0,2,1:T(8,128)(2,1)} %bitcast.31) | data formatting | bytes 7340032 | tf_op jit(solution)/shard_map/all_to_all | solution.py:34
  273.6 0.0 copy-done.2
  273.6 0.0 copy-start.5
  273.6 0.0 all-to-all-done.1
  273.6 6.0 %all-to-all-start = ((bf16[128,8,1792]{2,0,1:T(8,128)(2,1)}), bf16[128,8,1792]{2,0,1:T(8,128)(2,1)}, u32[]{:S(2)}, u32[]{:S(2)}) async-start(bf16[128,8,1792]{2,0,1:T(8,128)(2,1)} %copy.15), calls=%async_computation.1 | async-start | bytes 7340032 | tf_op jit(solution)/shard_map/all_to_all | solution.py:34
  279.6 0.1 add_select_fusion.2
  279.8 1.2 reduce-window.16
  280.9 0.2 slice_reduce_fusion.1
  281.2 0.1 bitcast_bitcast_fusion
  281.3 0.1 compare_and_fusion
  281.4 0.0 copy-done.5
  281.5 1.4 reshape.98
  282.9 2.7 gather_fusion.3
  285.6 1.4 reshape.94
  287.0 2.7 gather_fusion.1
  289.7 4.1 %add_convert_fusion = (bf16[448,1024]{1,0:T(8,128)(2,1)}, bf16[448,1024]{1,0:T(8,128)(2,1)}) fusion(bf16[448,1024]{1,0:T(8,128)(2,1)} %param.11, bf16[448,1024]{1,0:T(8,128)(2,1)} %gather_fusion.3, f32[448]{0:T(512)S(1)} %copy-done.5, f32[448]{0:T(512)S(1)} %broadcast_subtract_fusion, pred[448]{0:T(512)(128)(4,1)S(1)} %get-tuple-element.4, ...), kind=kLoop, calls=%fused_computation.13 | loop fusion | flops 6422528 | bytes 5509056 | tf_op jit(solution)/shard_map/convert_element_type | solution.py:12
  293.8 86.5 %all_gather.6 = bf16[1024,448]{0,1:T(8,128)(2,1)S(1)} all-gather(bf16[128,448]{0,1:T(8,128)(2,1)S(1)} %get-tuple-element.7), channel_id=1, replica_groups=mesh['fsdp'=32,'tok'=8] {'tok'}, dimensions={0}, use_global_device_ids=true | all-gather | bytes 1032192 | tf_op jit(solution)/shard_map/all_gather | solution.py:33
  380.4 0.0 all-to-all-done
  380.4 5.0 %multiply_convert_fusion = bf16[448,1792]{1,0:T(8,128)(2,1)} fusion(bf16[1024,448]{0,1:T(8,128)(2,1)S(1)} %all_gather.6, bf16[1024,1792]{1,0:T(8,128)(2,1)} %bitcast.3), kind=kOutput, calls=%fused_computation.12 | convolution fusion | flops 1645772800 | bytes 6193152 | tf_op jit(solution)/shard_map/dot_general | solution.py:35
  (17 shorter events, 0.3 us)
Async XLA Ops:
  7.2 1.6 copy-start
  7.2 96.1 %reduce-scatter.2.cloned.1.call-start = ((), (), s32[]{:S(2)}) async-start(), calls=%async_computation.4 | async-start | bytes 8257536 | tf_op jit(solution)/shard_map/reduce_scatter | solution.py:20
  17.8 87.6 %copy-start.4 = (s32[14336]{0:T(1024)S(1)}, s32[14336]{0:T(1024)}, u32[]{:S(2)}) copy-start(s32[14336]{0:T(1024)} %param.14) | copy-start | bytes 172036
  17.8 90.1 %copy-start.1 = (bf16[448,1024]{1,0:T(8,128)(2,1)S(1)}, bf16[448,1024]{1,0:T(8,128)(2,1)}, u32[]{:S(2)}) copy-start(bf16[448,1024]{1,0:T(8,128)(2,1)} %param.13) | copy-start | bytes 2752516
  17.8 249.9 %all-gather.2.cloned.1.call-start = ((), (), s32[]{:S(2)}) async-start(), calls=%async_computation.5 | async-start | bytes 3784704 | tf_op jit(solution)/shard_map/all_gather | solution.py:32
  110.6 4.8 %copy-start.3 = (bf16[448,1024]{1,0:T(8,128)(2,1)S(1)}, bf16[448,1024]{1,0:T(8,128)(2,1)}, u32[]{:S(2)}) copy-start(bf16[448,1024]{1,0:T(8,128)(2,1)} %gather_fusion.2) | copy-start | bytes 2752516
  120.2 27.0 %all-to-all-start.2 = ((bf16[32,14,1024]{2,1,0:T(8,128)(2,1)}), bf16[32,14,1024]{2,1,0:T(8,128)(2,1)S(1)}, u32[]{:S(2)}, u32[]{:S(2)}) async-start(bf16[32,14,1024]{2,1,0:T(8,128)(2,1)} %reshape.97), calls=%async_computation.3 | async-start | bytes 2097152 | tf_op jit(solution)/shard_map/all_to_all | solution.py:52
  147.3 126.4 %copy-start.2 = (bf16[32,14,1024]{2,1,0:T(8,128)(2,1)}, bf16[32,14,1024]{2,1,0:T(8,128)(2,1)S(1)}, u32[]{:S(2)}) copy-start(bf16[32,14,1024]{2,1,0:T(8,128)(2,1)S(1)} %all-to-all-done.2) | copy-start | bytes 2752516
  147.3 126.4 %all-to-all-start.1 = ((bf16[32,14,1024]{2,1,0:T(8,128)(2,1)}), bf16[32,14,1024]{2,1,0:T(8,128)(2,1)}, u32[]{:S(2)}, u32[]{:S(2)}) async-start(bf16[32,14,1024]{2,1,0:T(8,128)(2,1)} %reshape.93), calls=%async_computation.2 | async-start | bytes 2097152 | tf_op jit(solution)/shard_map/all_to_all | solution.py:51
  273.6 7.8 %copy-start.5 = (f32[448]{0:T(512)S(1)}, f32[448]{0:T(512)}, u32[]{:S(2)}) copy-start(f32[448]{0:T(512)} %param.15) | copy-start | bytes 5380
  273.6 106.7 %all-to-all-start = ((bf16[128,8,1792]{2,0,1:T(8,128)(2,1)}), bf16[128,8,1792]{2,0,1:T(8,128)(2,1)}, u32[]{:S(2)}, u32[]{:S(2)}) async-start(bf16[128,8,1792]{2,0,1:T(8,128)(2,1)} %copy.15), calls=%async_computation.1 | async-start | bytes 7340032 | tf_op jit(solution)/shard_map/all_to_all | solution.py:34
Sparse Core Ops, SparseCore 0:
  17.9 85.3 reduce-scatter.1
  105.5 162.1 all-gather.1
where the time goes:
time: 399 us; the launch traced here: 392 us
  waiting for transfers between devices  211 us (53%)
  blocking collectives  86.5 us (22%)
  local copies, waits for them, and re-layouts  28.8 us (7%)
  starting transfers between devices  25.3 us (6%)
  between operations  14.2 us (4%)
  matrix products  14 us (4%)
  other arithmetic  12 us (3%)
    all_gather x1, waiting for transfers between devices, body(): wide = lax.all_gather(act_b, 'fsdp', axis=1, tiled=True)  113 us
    all_gather x1, blocking collectives, body(): rows_a = lax.all_gather(act_a, 'tok', axis=0, tiled=True)  86.5 us
    reduce_scatter x1, waiting for transfers between devices, body(): lax.psum_scatter(lax.dot_general(tokens, stacked, contract, preferred_ele...  85.4 us
    all_to_all x1, waiting for transfers between devices, body(): lax.all_to_all(outgoing_up, 'fsdp', split_axis=0, concat_axis=0, tiled=True)  13.3 us
    all_to_all x1, starting transfers between devices, body(): lax.all_to_all(outgoing_up, 'fsdp', split_axis=0, concat_axis=0, tiled=True)  11.4 us
    dot_general x1, matrix products, body(): lax.dot_general(tokens, stacked, contract, preferred_element_type=jnp.flo...  8.99 us
  transfers between devices with their start and end apart: 5, of which 3 were waited for; matrix products, arithmetic and copies ran while one was open for 9% of the time, Pallas kernels for 0%

commit v1 on v0

v1 whole, which is shorter than its diff:
```python
import math

import jax
import jax.numpy as jnp
from jax import lax
from jax.experimental import pallas as pl
from jax.experimental.pallas import tpu as pltpu
from jax.sharding import PartitionSpec as P

MESH = pl.DeviceIdType.MESH
BF16, F32 = jnp.bfloat16, jnp.float32
UNITS = 448
HALF = UNITS // 2
WIDTH = 1024
QUARTER = 256
SLOTS = 16
NT = (((1,), (1,)), ((), ()))


def device(x, y, l, h, c):
    return (l * 16 + y * 4 + x, h * 2 + c)


def remote(src, dst, send, recv, to):
    return pltpu.make_async_remote_copy(
        src_ref=src, dst_ref=dst, send_sem=send, recv_sem=recv, device_id=to, device_id_type=MESH
    )


def rows(start, size, step):
    return pl.ds(pl.multiple_of(start, step), size)


def kernel(
    tok, gate_a, up_a, gate_b, up_b, send_rows, position, mixing,
    corr, merged_gate, merged_up,
    tk, wh, wb, wa, outb, inb, sb, rb, pa, pb, po, ab, aa, bb, acc, corr_v, mg_v, onehot,
    l_sem, xs_sem, xr_sem, as_sem, ar_sem, rs_s, rs_r, b1_s, b1_r, b2_s, b2_r, b3_s, b3_r,
    az_s, az_r, ac_s, ac_r, o_sem,
):
    f, t = lax.axis_index("fsdp"), lax.axis_index("tok")
    x, y, l = lax.rem(f, 4), lax.rem(lax.div(f, 4), 4), lax.div(f, 16)
    h, c = lax.div(t, 2), lax.rem(t, 2)
    weights = (gate_a, up_a, gate_b, up_b)
    order = [lax.rem(h + d, 4) for d in (2, 1, 3, 0)]

    loads = []
    for i, w in enumerate(weights):
        loads.append(
            pltpu.make_async_copy(
                w.at[rows(c * HALF, HALF, HALF)], wh.at[c, pl.ds(i * HALF, HALF)], l_sem.at[i]
            )
        )
    loads.append(pltpu.make_async_copy(tok, tk.at[c], l_sem.at[4]))
    loads_b = [
        pltpu.make_async_copy(w, wb.at[i], l_sem.at[5 + i]) for i, w in enumerate((gate_b, up_b))
    ]
    loads_a = [
        pltpu.make_async_copy(w, wa.at[i], l_sem.at[7 + i]) for i, w in enumerate((gate_a, up_a))
    ]
    for cp in loads + loads_b + loads_a:
        cp.start()

    barrier = pltpu.get_barrier_semaphore()

    def greet_f(i, carry):
        pl.semaphore_signal(
            barrier, inc=1, device_id=(lax.rem(f + i, 32), t), device_id_type=MESH
        )
        return carry

    def greet_t(i, carry):
        other = lax.rem(t + i, 8)
        pl.semaphore_signal(barrier, inc=1, device_id=(f, other), device_id_type=MESH)
        pl.semaphore_signal(
            barrier, inc=1, device_id=(lax.rem(f + 16, 32), other), device_id_type=MESH
        )
        return carry

    lax.fori_loop(1, 32, greet_f, 0)
    lax.fori_loop(1, 8, greet_t, 0)
    pl.semaphore_wait(barrier, 45)

    sibling = (f, t + 1 - 2 * c)
    swaps = []
    for i, w in enumerate(weights):
        swaps.append(
            remote(
                w.at[rows((1 - c) * HALF, HALF, HALF)],
                wh.at[c, pl.ds(i * HALF, HALF)],
                xs_sem.at[i],
                xr_sem.at[i],
                sibling,
            )
        )
    for i, e in enumerate(order):
        part = rows(e * QUARTER, QUARTER, QUARTER)
        swaps.append(
            remote(tok.at[part], tk.at[c, part], xs_sem.at[4 + i], xr_sem.at[4 + i], sibling)
        )
    for cp in swaps:
        cp.start()

    onehot[...] = (
        lax.broadcasted_iota(jnp.int32, (32 * SLOTS, UNITS), 1) == send_rows[...]
    ).astype(F32).astype(BF16)
    for i in range(2):
        loads_b[i].wait()
        picked = jnp.dot(onehot[...], wb[i], preferred_element_type=F32).astype(BF16)
        outb[:, i * SLOTS : (i + 1) * SLOTS, :] = picked.reshape(32, SLOTS, WIDTH)

    own_rows = pltpu.make_async_copy(outb.at[f], inb.at[f], l_sem.at[9])
    own_rows.start()

    def a2a(i):
        to = lax.rem(f + i, 32)
        return remote(outb.at[to], inb.at[f], as_sem.at[i], ar_sem.at[i], (to, t))

    def a2a_in(i):
        frm = lax.rem(f + 32 - i, 32)
        return remote(outb.at[frm], inb.at[frm], as_sem.at[i], ar_sem.at[i], (frm, t))

    def plane_step(i, carry):
        to = l * 16 + lax.rem(lax.rem(f, 16) + i, 16)
        a2a(lax.rem(to - f + 32, 32)).start()
        return carry

    def cross_step(i, carry):
        to = (1 - l) * 16 + lax.rem(lax.rem(f, 16) + i, 16)
        a2a(lax.rem(to - f + 32, 32)).start()
        return carry

    lax.fori_loop(1, 16, plane_step, 0)

    for cp in loads:
        cp.wait()
    for cp in swaps[:4]:
        cp.wait_recv()

    def partial(i):
        swaps[4 + i].wait_recv()
        part = rows(order[i] * QUARTER, QUARTER, QUARTER)
        return lax.dot_general(
            wh[0], tk[0, part, :], NT, preferred_element_type=F32
        ) + lax.dot_general(wh[1], tk[1, part, :], NT, preferred_element_type=F32)

    plus = device(x, y, l, lax.rem(h + 1, 4), c)
    minus = device(x, y, l, lax.rem(h + 3, 4), c)

    def ring(i, to):
        return remote(sb.at[i], rb.at[i], rs_s.at[i], rs_r.at[i], to)

    far_a, far_b, near_b, near_a = ring(0, plus), ring(1, minus), ring(2, plus), ring(3, minus)
    acc_a, acc_b = ring(4, plus), ring(5, minus)

    p = partial(0)
    sb[1] = p[UNITS:].astype(BF16)
    far_b.start()
    sb[0] = p[:UNITS].astype(BF16)
    far_a.start()
    p = partial(1)
    sb[2] = p[UNITS:].astype(BF16)
    near_b.start()
    pa[...] = p[:UNITS]
    p = partial(2)
    sb[3] = p[:UNITS].astype(BF16)
    near_a.start()
    pb[...] = p[UNITS:]
    po[...] = partial(3)
    far_b.wait_recv()
    sb[5] = (pb[...] + rb[1].astype(F32)).astype(BF16)
    acc_b.start()
    far_a.wait_recv()
    sb[4] = (pa[...] + rb[0].astype(F32)).astype(BF16)
    acc_a.start()

    lax.fori_loop(0, 16, cross_step, 0)

    def activation(lo, first, second):
        total = po[lo : lo + UNITS, :] + rb[first].astype(F32) + rb[second].astype(F32)
        gate, up = total[:HALF], total[HALF:]
        return ((gate / (1.0 + jnp.exp(-gate))) * up).astype(BF16)

    near_b.wait_recv()
    acc_b.wait_recv()
    ab[...] = activation(UNITS, 2, 5)
    slab, side = 2 * l + lax.div(y, 2), lax.rem(y, 2)
    mine = rows(x * UNITS + c * HALF, HALF, HALF)
    b1_slot = h * 2 + c
    to_root = remote(
        ab, bb.at[h, mine], b1_s.at[0], b1_r.at[b1_slot], device(x, y, l, slab, side)
    )
    to_twin = remote(
        ab, bb.at[h, mine], b1_s.at[1], b1_r.at[b1_slot], device(x, y, 1 - l, slab, side)
    )
    is_self = jnp.logical_and(slab == h, side == c)
    to_twin.start()

    @pl.when(jnp.logical_not(is_self))
    def _():
        to_root.start()

    @pl.when(is_self)
    def _():
        pltpu.make_async_copy(ab, bb.at[h, mine], b1_r.at[b1_slot]).start()

    near_a.wait_recv()
    acc_a.wait_recv()
    half = rows(c * HALF, HALF, HALF)
    aa[h, half, :] = activation(0, 3, 4)
    a_out = [
        remote(
            aa.at[h, half], aa.at[h, half], az_s.at[d], az_r.at[d],
            device(x, y, l, lax.rem(h + d, 4), c),
        )
        for d in (1, 3, 2)
    ]
    for cp in a_out:
        cp.start()

    def a_in(d):
        frm = lax.rem(h + 4 - d, 4)
        return remote(
            aa.at[frm, half], aa.at[frm, half], az_s.at[d], az_r.at[d], device(x, y, l, frm, c)
        )

    def relay(d):
        frm = lax.rem(h + 4 - d, 4)
        return remote(aa.at[frm, half], aa.at[frm, half], ac_s.at[d], ac_r.at[d], sibling)

    def relay_in(d):
        frm = lax.rem(h + 4 - d, 4)
        other = rows((1 - c) * HALF, HALF, HALF)
        return remote(aa.at[frm, other], aa.at[frm, other], ac_s.at[d], ac_r.at[d], sibling)

    relay(0).start()

    is_root = y == 2 * lax.rem(h, 2) + c
    right = device(lax.rem(x + 1, 4), y, l, h, c)
    left = device(lax.rem(x + 3, 4), y, l, h, c)
    quarters = [lax.rem(h + d, 4) for d in (0, 1, 3, 2)]

    def block(q, dx):
        return bb.at[q, rows(lax.rem(x + dx, 4) * UNITS, UNITS, UNITS)]

    def down(s, dy):
        here = block(quarters[s], 0)
        return remote(
            here, here, b2_s.at[s, dy - 1], b2_r.at[s], device(x, lax.rem(y + dy, 4), l, h, c)
        )

    def to_right(s):
        here = block(quarters[s], 0)
        return remote(here, here, b3_s.at[s, 0], b3_r.at[s, 0], right)

    def to_left(s):
        here = block(quarters[s], 0)
        return remote(here, here, b3_s.at[s, 1], b3_r.at[s, 1], left)

    def from_left(s):
        there = block(quarters[s], 3)
        return remote(there, there, b3_s.at[s, 0], b3_r.at[s, 0], left)

    def from_right(s):
        there = block(quarters[s], 1)
        return remote(there, there, b3_s.at[s, 1], b3_r.at[s, 1], right)

    def forward(s):
        there = block(quarters[s], 3 if s % 2 == 0 else 1)
        return remote(there, there, b3_s.at[s, 2], b3_r.at[s, 2], right if s % 2 == 0 else left)

    def from_far(s):
        there = block(quarters[s], 2)
        return remote(there, there, b3_s.at[s, 2], b3_r.at[s, 2], left if s % 2 == 0 else right)

    def b1_in(s, core):
        q = quarters[s]
        here = bb.at[q, rows(x * UNITS + core * HALF, HALF, HALF)]
        return pltpu.make_async_copy(here, here, b1_r.at[q * 2 + core])

    def correlate(s):
        term = lax.dot_general(
            aa[quarters[s]], bb[quarters[s]], NT, preferred_element_type=F32
        )
        if s == 0:
            acc[...] = term
        elif s < 3:
            acc[...] += term
        else:
            corr_v[...] = ((acc[...] + term) * (1.0 / 32.0)).astype(BF16)

    relayed = [0, 3, 1, 2]
    for step in range(6):
        if step < 4:

            @pl.when(is_root)
            def _():
                b1_in(step, 0).wait()
                b1_in(step, 1).wait()
                for dy in (1, 3, 2):
                    down(step, dy).start()

            @pl.when(jnp.logical_not(is_root))
            def _():
                down(step, 1).wait_recv()

            to_right(step).start()
            to_left(step).start()
        if step == 1:
            for d in (1, 3):
                a_in(d).wait_recv()
                relay(d).start()
        if step == 2:
            a_in(2).wait_recv()
            relay(2).start()
        if 1 <= step < 5:
            from_left(step - 1).wait_recv()
            from_right(step - 1).wait_recv()
            forward(step - 1).start()
        if step == 5:
            own_rows.wait()

            def arrived(i, carry):
                a2a_in(i).wait_recv()
                return carry

            lax.fori_loop(1, 32, arrived, 0)
            for cp in loads_a:
                cp.wait()
            weight = mixing[...]
            lane = lax.broadcasted_iota(jnp.int32, (UNITS, 32 * 2 * SLOTS), 1)
            received = inb[...].reshape(32 * 2 * SLOTS, WIDTH)
            for i, out in enumerate((merged_gate, merged_up)):
                pick = (lane == position[...] + i * SLOTS).astype(F32).astype(BF16)
                got = jnp.dot(pick, received, preferred_element_type=F32)
                mg_v[i] = ((1.0 - weight) * wa[i].astype(F32) + weight * got).astype(BF16)
                pltpu.make_async_copy(mg_v.at[i], out, o_sem.at[i]).start()
        if step >= 2:
            if step == 2:
                relay_in(0).wait_recv()
                for d in (1, 3, 2):
                    relay_in(d).wait_recv()
            from_far(step - 2).wait_recv()
            correlate(step - 2)

    out = pltpu.make_async_copy(corr_v, corr, o_sem.at[2])
    out.start()

    for cp in swaps + [far_a, far_b, near_a, near_b, acc_a, acc_b, to_twin] + a_out:
        cp.wait_send()

    @pl.when(jnp.logical_not(is_self))
    def _():
        to_root.wait_send()

    for s in range(4):

        @pl.when(is_root)
        def _():
            for dy in (1, 3, 2):
                down(s, dy).wait_send()

        to_right(s).wait_send()
        to_left(s).wait_send()
        forward(s).wait_send()
        relay(s).wait_send()

    def left_all(i, carry):
        a2a(i).wait_send()
        return carry

    lax.fori_loop(1, 32, left_all, 0)
    pltpu.make_async_copy(mg_v.at[0], merged_gate, o_sem.at[0]).wait()
    pltpu.make_async_copy(mg_v.at[1], merged_up, o_sem.at[1]).wait()
    out.wait()


def body(tokens, gate_a, up_a, gate_b, up_b, matching, mixing):
    count = lax.axis_size("fsdp")
    own = lax.axis_index("fsdp")
    table = matching.reshape(count, UNITS)
    chosen = (table // UNITS == own).astype(jnp.int32)
    slot = jnp.cumsum(chosen, axis=1) - 1
    hits = jnp.logical_and(
        chosen[:, None, :] > 0, slot[:, None, :] == jnp.arange(SLOTS)[None, :, None]
    )
    send_rows = jnp.sum(jnp.where(hits, (table % UNITS)[:, None, :], 0), axis=2).reshape(-1, 1)
    wanted = lax.dynamic_slice_in_dim(matching, own * UNITS, UNITS, 0)
    anchor = wanted // UNITS
    same = (anchor[:, None] == jnp.arange(count)[None, :]).astype(jnp.int32)
    rank = jnp.sum(same * (jnp.cumsum(same, axis=0) - 1), axis=1)
    position = (anchor * (2 * SLOTS) + rank).reshape(-1, 1)

    any_space = pl.BlockSpec(memory_space=pl.ANY)
    vmem = pl.BlockSpec(memory_space=pltpu.VMEM)
    dma = pltpu.SemaphoreType.DMA
    return pl.pallas_call(
        kernel,
        name="match_merge",
        out_shape=(
            jax.ShapeDtypeStruct((UNITS, 4 * UNITS), BF16),
            jax.ShapeDtypeStruct((UNITS, WIDTH), BF16),
            jax.ShapeDtypeStruct((UNITS, WIDTH), BF16),
        ),
        in_specs=[any_space] * 5 + [vmem] * 3,
        out_specs=(any_space,) * 3,
        scratch_shapes=[
            pltpu.VMEM((2, 1024, WIDTH), BF16),
            pltpu.VMEM((2, 4 * HALF, WIDTH), BF16),
            pltpu.VMEM((2, UNITS, WIDTH), BF16),
            pltpu.VMEM((2, UNITS, WIDTH), BF16),
            pltpu.VMEM((32, 2 * SLOTS, WIDTH), BF16),
            pltpu.VMEM((32, 2 * SLOTS, WIDTH), BF16),
            pltpu.VMEM((6, UNITS, QUARTER), BF16),
            pltpu.VMEM((6, UNITS, QUARTER), BF16),
            pltpu.VMEM((UNITS, QUARTER), F32),
            pltpu.VMEM((UNITS, QUARTER), F32),
            pltpu.VMEM((2 * UNITS, QUARTER), F32),
            pltpu.VMEM((HALF, QUARTER), BF16),
            pltpu.VMEM((4, UNITS, QUARTER), BF16),
            pltpu.VMEM((4, 4 * UNITS, QUARTER), BF16),
            pltpu.VMEM((UNITS, 4 * UNITS), F32),
            pltpu.VMEM((UNITS, 4 * UNITS), BF16),
            pltpu.VMEM((2, UNITS, WIDTH), BF16),
            pltpu.VMEM((32 * SLOTS, UNITS), BF16),
            dma((10,)),
            dma((8,)),
            dma((8,)),
            dma((32,)),
            dma((32,)),
            dma((6,)),
            dma((6,)),
            dma((2,)),
            dma((8,)),
            dma((4, 3)),
            dma((4,)),
            dma((4, 3)),
            dma((4, 3)),
            dma((4,)),
            dma((4,)),
            dma((4,)),
            dma((4,)),
            dma((3,)),
        ],
        compiler_params=pltpu.CompilerParams(
            collective_id=0, has_side_effects=True, vmem_limit_bytes=56 * 2**20
        ),
        cost_estimate=pl.CostEstimate(
            flops=8_000_000_000, bytes_accessed=20_000_000, transcendentals=500_000
        ),
    )(tokens, gate_a, up_a, gate_b, up_b, send_rows, position, mixing.reshape(-1, 1))


def solution(mesh):
    placed = (
        P(None, "tok"),
        P("fsdp", "tok"),
        P("fsdp", "tok"),
        P("fsdp", "tok"),
        P("fsdp", "tok"),
        P(),
        P("fsdp"),
    )
    return jax.shard_map(
        body,
        mesh=mesh,
        in_specs=placed,
        out_specs=(P("fsdp", "tok"), P("fsdp", "tok"), P("fsdp", "tok")),
        check_vma=False,
    )
```

time: 399 us -> 139 us (0.35); the launches traced: 392 us -> 139 us
  waiting for transfers between devices: 211 us -> 0 us
  Pallas kernels: 0 us -> 123 us
  blocking collectives: 86.5 us -> 0 us
  starting transfers between devices: 25.3 us -> 0 us
  local copies, waits for them, and re-layouts: 28.8 us -> 8.45 us
  matrix products: 14 us -> 0 us
  between operations: 14.2 us -> 0.73 us
  other arithmetic: 12 us -> 6.59 us
    pallas_call x0 -> x1, Pallas kernels: none -> 123 us  [body(): pl.pallas_call(kernel, name='match_merge', out_shape=(jax.ShapeDtypeStruc...]
    all_gather x1 -> x0, waiting for transfers between devices: 113 us -> none  [body(): wide = lax.all_gather(act_b, 'fsdp', axis=1, tiled=True)]
    all_gather x1 -> x0, blocking collectives: 86.5 us -> none  [body(): rows_a = lax.all_gather(act_a, 'tok', axis=0, tiled=True)]
    reduce_scatter x1 -> x0, waiting for transfers between devices: 85.4 us -> none  [body(): lax.psum_scatter(lax.dot_general(tokens, stacked, contract, preferred_ele...]
    all_to_all x3 -> x0, starting transfers between devices: 25.3 us -> none  [the longest x1 11.4 us: body(): lax.all_to_all(outgoing_up, 'fsdp', split_axis=0, concat_axis=0, tiled=True)]
    dot_general x2 -> x0, matrix products: 14 us -> none  [the longest x1 8.99 us: body(): lax.dot_general(tokens, stacked, contract, preferred_element_type=jnp.flo...]
    all_to_all x3 -> x0, waiting for transfers between devices: 13.4 us -> none  [the longest x1 13.3 us: body(): lax.all_to_all(outgoing_up, 'fsdp', split_axis=0, concat_axis=0, tiled=True)]
    gather x4 -> x0, local copies, waits for them, and re-layouts: 13 us -> none  [the longest x1 4.8 us: body(): jnp.take(gate_b, send_rows, axis=0).reshape(fsdp_count, capacity, -1)]
  transfers between devices with their start and end apart: 5 -> 0, of which waited for: 3 -> 0; matrix products, arithmetic and copies ran while one was open for 9% -> 0% of each run, Pallas kernels for 0% -> 0%
where the time goes in v1:
time: 139 us
  Pallas kernels  123 us (88%)
  local copies, waits for them, and re-layouts  8.45 us (6%)
  other arithmetic  6.59 us (5%)
    pallas_call x1, Pallas kernels, body(): pl.pallas_call(kernel, name='match_merge', out_shape=(jax.ShapeDtypeStruc...  123 us
    unnamed x9, local copies, waits for them, and re-layouts  5.2 us

profile of v1, /device:TPU:56, one launch (start us, length us, event | category | flops | bytes accessed | tf_op | source)
XLA Modules:
  0.0 138.6 jit_solution(2846574306005613865)
XLA Ops:
  0.6 0.0 copy-start.2
  0.6 0.8 add_select_fusion.2
  1.4 0.8 sign_compare_fusion
  2.3 0.1 ne.58
  2.4 1.2 reduce-window.16
  3.6 0.2 slice_reduce_fusion
  3.8 0.1 bitcast_bitcast_fusion
  4.0 0.8 multiply_add_fusion
  4.8 0.9 broadcast_divide_fusion
  5.6 0.1 div.20
  5.7 0.1 rem.34
  5.8 1.2 reduce-window.14
  7.0 0.2 slice_reduce_fusion.1
  7.3 0.1 copy_bitcast_fusion
  7.4 0.6 select_reduce_fusion
  8.0 0.8 copy.22.position
  8.9 0.0 copy-done.2
  8.9 0.8 copy.23.mixing
  9.7 0.9 reshape.83.send_rows
  10.6 122.9 %match_merge.1 = (bf16[448,1792]{1,0:T(8,128)(2,1)}, bf16[448,1024]{1,0:T(8,128)(2,1)}, bf16[448,1024]{1,0:T(8,128)(2,1)}) custom-call(bf16[1024,1024]{1,0:T(8,128)(2,1)} %tok.1, bf16[448,1024]{1,0:T(8,128)(2,1)} %gate_a.1, bf16[448,1024]{1,0:T(8,128)(2,1)} %up_a.1, bf16[448,1024]{1,0:T(8,128)(2,1)} %gate_b.1, bf16[448,1024]{1,0:T(8,128)(2,1)} %up_b.1, ...), custom_call_target="tpu_custom_call" | custom-call | flops 8000000000 | bytes 20000000 | tf_op jit(solution)/shard_map/match_merge/pallas_call | solution.py:397
  133.4 0.0 copy-start.1
  133.5 2.8 %copy.35 = bf16[448,1792]{1,0:T(8,128)(2,1)} copy(bf16[448,1792]{1,0:T(8,128)(2,1)} %get-tuple-element.12) | data formatting | bytes 3211264
  136.2 0.0 copy-done.1
  136.2 0.0 copy-start
  136.2 0.9 copy.36
  137.1 0.6 copy-done
  137.7 0.9 copy.37
  (10 shorter events, 0.2 us)
Async XLA Ops:
  0.6 8.2 %copy-start.2 = (f32[448]{0:T(512)S(1)}, f32[448]{0:T(512)}, u32[]{:S(2)}) copy-start(f32[448]{0:T(512)} %param.13) | copy-start | bytes 5380
  133.4 2.8 %copy-start.1 = (bf16[448,1024]{1,0:T(8,128)(2,1)S(1)}, bf16[448,1024]{1,0:T(8,128)(2,1)}, u32[]{:S(2)}) copy-start(bf16[448,1024]{1,0:T(8,128)(2,1)} %get-tuple-element.13) | copy-start | bytes 2752516
  136.2 1.5 %copy-start = (bf16[448,1024]{1,0:T(8,128)(2,1)S(1)}, bf16[448,1024]{1,0:T(8,128)(2,1)}, u32[]{:S(2)}) copy-start(bf16[448,1024]{1,0:T(8,128)(2,1)} %get-tuple-element.14) | copy-start | bytes 2752516

commit v2 on v1

v2 whole, which is shorter than its diff:
```python
import jax
import jax.numpy as jnp
from jax import lax
from jax.experimental import pallas as pl
from jax.experimental.pallas import tpu as pltpu
from jax.sharding import PartitionSpec as P

MESH = pl.DeviceIdType.MESH
BF16, F32 = jnp.bfloat16, jnp.float32
UNITS = 448
HALF = UNITS // 2
WIDTH = 1024
QUARTER = 256
SLOTS = 16
NT = (((1,), (1,)), ((), ()))


def device(x, y, l, h, c):
    return (l * 16 + y * 4 + x, h * 2 + c)


def remote(src, dst, send, recv, to):
    return pltpu.make_async_remote_copy(
        src_ref=src, dst_ref=dst, send_sem=send, recv_sem=recv, device_id=to, device_id_type=MESH
    )


def rows(start, size, step):
    return pl.ds(pl.multiple_of(start, step), size)


def kernel(
    tok, gate_a, up_a, gate_b, up_b, table, mixing,
    corr, merged_gate, merged_up,
    tk, wh, wb, wa, outb, near_in, twin_in, sb, rb, keep, ab, aa, bb, acc, corr_v, mg_v,
    send_hot, take_hot, line, column,
    l_sem, xs_s, xs_r, as_s, as_r, fw_s, fw_r, rs_s, rs_r, b1_s, b1_r, b2_s, b2_r, b3_s, b3_r,
    az_s, az_r, ac_s, ac_r, o_sem,
):
    f, t = lax.axis_index("fsdp"), lax.axis_index("tok")
    x, y, l = lax.rem(f, 4), lax.rem(lax.div(f, 4), 4), lax.div(f, 16)
    h, c = lax.div(t, 2), lax.rem(t, 2)
    xy = lax.rem(f, 16)
    weights = (gate_b, up_b, gate_a, up_a)
    order = [lax.rem(h + d, 4) for d in (2, 1, 3, 0)]
    sibling = (f, t + 1 - 2 * c)
    twin = device(x, y, 1 - l, h, c)

    barrier = pltpu.get_barrier_semaphore()

    def greet_plane(i, carry):
        pl.semaphore_signal(
            barrier, inc=1, device_id=(l * 16 + lax.rem(xy + i, 16), t), device_id_type=MESH
        )
        return carry

    def greet_tok(i, carry):
        other = lax.rem(t + i, 8)
        pl.semaphore_signal(barrier, inc=1, device_id=(f, other), device_id_type=MESH)
        pl.semaphore_signal(
            barrier, inc=1, device_id=((1 - l) * 16 + xy, other), device_id_type=MESH
        )
        return carry

    lax.fori_loop(1, 16, greet_plane, 0)
    lax.fori_loop(1, 8, greet_tok, 0)
    pl.semaphore_signal(barrier, inc=1, device_id=twin, device_id_type=MESH)

    loads = []
    for i, w in enumerate(weights):
        loads.append(
            pltpu.make_async_copy(
                w.at[rows(c * HALF, HALF, HALF)], wh.at[c, pl.ds(i * HALF, HALF)], l_sem.at[i]
            )
        )
    load_tok = pltpu.make_async_copy(tok, tk.at[c], l_sem.at[4])
    loads_b = [
        pltpu.make_async_copy(w, wb.at[i], l_sem.at[5 + i]) for i, w in enumerate((gate_b, up_b))
    ]
    loads_a = [
        pltpu.make_async_copy(w, wa.at[i], l_sem.at[7 + i]) for i, w in enumerate((gate_a, up_a))
    ]
    for cp in loads_b + loads[:2] + [load_tok] + loads[2:] + loads_a:
        cp.start()

    low = f * UNITS
    value = table[...]
    local = value - low
    chosen = jnp.logical_and(local >= 0, local < UNITS)
    source = lax.broadcasted_iota(jnp.int32, (32, UNITS), 0)
    wanted = table[pl.ds(f, 1), :] - source * UNITS
    same = jnp.logical_and(wanted >= 0, wanted < UNITS)
    before = (
        lax.broadcasted_iota(jnp.int32, (UNITS, UNITS), 0)
        < lax.broadcasted_iota(jnp.int32, (UNITS, UNITS), 1)
    ).astype(F32).astype(BF16)
    chosen_f, same_f = chosen.astype(F32), same.astype(F32)
    rank = jnp.dot(chosen_f.astype(BF16), before, preferred_element_type=F32)
    rank_in = jnp.dot(same_f.astype(BF16), before, preferred_element_type=F32)
    base = (lax.rem(source + 16 * l, 32) * SLOTS).astype(F32)
    line[...] = jnp.zeros_like(line)
    line[0:1, 0:UNITS] = jnp.sum(same_f * (base + rank_in), axis=0, keepdims=True)
    line[1:2, 0:UNITS] = mixing[...]
    column[...] = line[...].T
    take_hot[...] = (
        lax.broadcasted_iota(jnp.int32, (UNITS, 32 * SLOTS), 1)
        == column[0:UNITS, 0:1].astype(jnp.int32)
    ).astype(F32).astype(BF16)
    slot_row = lax.broadcasted_iota(jnp.int32, (32 * SLOTS, 32), 0)
    to_block = lax.rem(lax.broadcasted_iota(jnp.int32, (32 * SLOTS, 32), 1) + 16 * l, 32)
    spread = (lax.shift_right_logical(slot_row, 4) == to_block).astype(F32).astype(BF16)

    def widen(v):
        return jnp.dot(spread, v.astype(BF16), preferred_element_type=F32)

    code = widen(chosen_f * (rank + 1.0) - 1.0)
    high = widen(chosen_f * lax.shift_right_arithmetic(local, 4).astype(F32))
    lowp = widen(chosen_f * jnp.bitwise_and(local, 15).astype(F32))
    slot = jnp.bitwise_and(
        lax.broadcasted_iota(jnp.int32, (32 * SLOTS, UNITS), 0), SLOTS - 1
    ).astype(F32)
    picked_row = jnp.sum(
        jnp.where(code == slot, high * 16.0 + lowp, 0.0), axis=1, keepdims=True
    ).astype(jnp.int32)
    send_hot[...] = (
        lax.broadcasted_iota(jnp.int32, (32 * SLOTS, UNITS), 1) == picked_row
    ).astype(F32).astype(BF16)

    pl.semaphore_wait(barrier, 30)

    swaps = []
    for i, w in enumerate(weights):
        swaps.append(
            remote(
                w.at[rows((1 - c) * HALF, HALF, HALF)],
                wh.at[c, pl.ds(i * HALF, HALF)],
                xs_s.at[i],
                xs_r.at[i],
                sibling,
            )
        )
    for i, e in enumerate(order):
        part = rows(e * QUARTER, QUARTER, QUARTER)
        swaps.append(
            remote(tok.at[part], tk.at[c, part], xs_s.at[4 + i], xs_r.at[4 + i], sibling)
        )
    for i in (0, 1, 4, 5, 6, 7, 2, 3):
        swaps[i].start()

    for i in range(2):
        loads_b[i].wait()
        picked = jnp.dot(send_hot[...], wb[i], preferred_element_type=F32).astype(BF16)
        outb[:, 0, i] = picked[: 16 * SLOTS].reshape(16, SLOTS, WIDTH)
        outb[:, 1, i] = picked[16 * SLOTS :].reshape(16, SLOTS, WIDTH)

    def plane(i):
        to = lax.rem(xy + i, 16)
        return remote(outb.at[to], near_in.at[xy], as_s.at[i], as_r.at[i], (l * 16 + to, t))

    def plane_in(i):
        frm = lax.rem(xy + 16 - i, 16)
        return remote(outb.at[frm], near_in.at[frm], as_s.at[i], as_r.at[i], (l * 16 + frm, t))

    def plane_step(i, carry):
        plane(i).start()
        return carry

    own_rows = pltpu.make_async_copy(outb.at[xy, 0], near_in.at[xy, 0], l_sem.at[9])
    own_rows.start()
    own_cross = remote(outb.at[xy, 1], twin_in.at[xy], fw_s.at[0], fw_r.at[0], twin)
    lax.fori_loop(1, 16, plane_step, 0)

    plus = device(x, y, l, lax.rem(h + 1, 4), c)
    minus = device(x, y, l, lax.rem(h + 3, 4), c)

    def ring(k, i):
        return remote(
            sb.at[k, i], rb.at[k, i], rs_s.at[k, i], rs_r.at[k, i], plus if i % 2 == 0 else minus
        )

    def partial(k, i):
        part = rows(order[i] * QUARTER, QUARTER, QUARTER)
        mine = slice(k * UNITS, (k + 1) * UNITS)
        return lax.dot_general(
            wh[0, mine], tk[0, part, :], NT, preferred_element_type=F32
        ) + lax.dot_general(wh[1, mine], tk[1, part, :], NT, preferred_element_type=F32)

    def push(k, i, v):
        sb[k, i] = v.astype(BF16)
        ring(k, i).start()

    for cp in loads[:2] + [load_tok]:
        cp.wait()
    for i in (0, 1, 4):
        swaps[i].wait_recv()
    p = partial(0, 0)
    push(0, 0, p[:HALF])
    push(0, 1, p[HALF:])
    swaps[5].wait_recv()
    p = partial(0, 1)
    push(0, 2, p[HALF:])
    keep[0, 0] = p[:HALF]
    swaps[6].wait_recv()
    p = partial(0, 2)
    push(0, 3, p[:HALF])
    keep[0, 1] = p[HALF:]
    swaps[7].wait_recv()
    p = partial(0, 3)
    keep[0, 2] = p[:HALF]
    keep[0, 3] = p[HALF:]
    for cp in loads[2:]:
        cp.wait()
    for i in (2, 3):
        swaps[i].wait_recv()
    p = partial(1, 0)
    sb[1, 0] = p[:HALF].astype(BF16)
    sb[1, 1] = p[HALF:].astype(BF16)
    for i in range(2):
        ring(0, i).wait_recv()
        push(0, 4 + i, keep[0, i] + rb[0, i].astype(F32))
    ring(1, 0).start()
    ring(1, 1).start()
    p = partial(1, 1)
    push(1, 2, p[HALF:])
    keep[1, 0] = p[:HALF]
    p = partial(1, 2)
    push(1, 3, p[:HALF])
    keep[1, 1] = p[HALF:]
    p = partial(1, 3)
    keep[1, 2] = p[:HALF]
    keep[1, 3] = p[HALF:]

    def activation(k):
        for i in range(2, 6):
            ring(k, i).wait_recv()
        gate = keep[k, 2] + rb[k, 3].astype(F32) + rb[k, 4].astype(F32)
        up = keep[k, 3] + rb[k, 2].astype(F32) + rb[k, 5].astype(F32)
        return ((gate / (1.0 + jnp.exp(-gate))) * up).astype(BF16)

    ab[...] = activation(0)
    slab, side = 2 * l + lax.div(y, 2), lax.rem(y, 2)
    mine = rows(x * UNITS + c * HALF, HALF, HALF)
    b1_slot = h * 2 + c
    to_root = remote(
        ab, bb.at[h, mine], b1_s.at[0], b1_r.at[b1_slot], device(x, y, l, slab, side)
    )
    to_twin = remote(
        ab, bb.at[h, mine], b1_s.at[1], b1_r.at[b1_slot], device(x, y, 1 - l, slab, side)
    )
    is_self = jnp.logical_and(slab == h, side == c)
    to_twin.start()

    @pl.when(jnp.logical_not(is_self))
    def _():
        to_root.start()

    @pl.when(is_self)
    def _():
        pltpu.make_async_copy(ab, bb.at[h, mine], b1_r.at[b1_slot]).start()

    for i in range(2):
        ring(1, i).wait_recv()
        push(1, 4 + i, keep[1, i] + rb[1, i].astype(F32))

    half = rows(c * HALF, HALF, HALF)
    a_out = [
        remote(
            aa.at[h, half], aa.at[h, half], az_s.at[d], az_r.at[d],
            device(x, y, l, lax.rem(h + d, 4), c),
        )
        for d in (1, 3, 2)
    ]

    def a_in(d):
        frm = lax.rem(h + 4 - d, 4)
        return remote(
            aa.at[frm, half], aa.at[frm, half], az_s.at[d], az_r.at[d], device(x, y, l, frm, c)
        )

    def relay(d):
        frm = lax.rem(h + 4 - d, 4)
        return remote(aa.at[frm, half], aa.at[frm, half], ac_s.at[d], ac_r.at[d], sibling)

    def relay_in(d):
        frm = lax.rem(h + 4 - d, 4)
        other = rows((1 - c) * HALF, HALF, HALF)
        return remote(aa.at[frm, other], aa.at[frm, other], ac_s.at[d], ac_r.at[d], sibling)

    is_root = y == 2 * lax.rem(h, 2) + c
    right = device(lax.rem(x + 1, 4), y, l, h, c)
    left = device(lax.rem(x + 3, 4), y, l, h, c)
    quarters = [lax.rem(h + d, 4) for d in (0, 1, 3, 2)]

    def block(q, dx):
        return bb.at[q, rows(lax.rem(x + dx, 4) * UNITS, UNITS, UNITS)]

    def down(s, dy):
        here = block(quarters[s], 0)
        return remote(
            here, here, b2_s.at[s, dy - 1], b2_r.at[s], device(x, lax.rem(y + dy, 4), l, h, c)
        )

    def to_right(s):
        here = block(quarters[s], 0)
        return remote(here, here, b3_s.at[s, 0], b3_r.at[s, 0], right)

    def to_left(s):
        here = block(quarters[s], 0)
        return remote(here, here, b3_s.at[s, 1], b3_r.at[s, 1], left)

    def from_left(s):
        there = block(quarters[s], 3)
        return remote(there, there, b3_s.at[s, 0], b3_r.at[s, 0], left)

    def from_right(s):
        there = block(quarters[s], 1)
        return remote(there, there, b3_s.at[s, 1], b3_r.at[s, 1], right)

    def forward(s):
        there = block(quarters[s], 3 if s % 2 == 0 else 1)
        return remote(there, there, b3_s.at[s, 2], b3_r.at[s, 2], right if s % 2 == 0 else left)

    def from_far(s):
        there = block(quarters[s], 2)
        return remote(there, there, b3_s.at[s, 2], b3_r.at[s, 2], left if s % 2 == 0 else right)

    def b1_in(s, core):
        q = quarters[s]
        here = bb.at[q, rows(x * UNITS + core * HALF, HALF, HALF)]
        return pltpu.make_async_copy(here, here, b1_r.at[q * 2 + core])

    def correlate(s):
        term = lax.dot_general(
            aa[quarters[s]], bb[quarters[s]], NT, preferred_element_type=F32
        )
        if s == 0:
            acc[...] = term
        elif s < 3:
            acc[...] += term
        else:
            corr_v[...] = ((acc[...] + term) * (1.0 / 32.0)).astype(BF16)

    def spread_out(s):
        @pl.when(is_root)
        def _():
            b1_in(s, 0).wait()
            b1_in(s, 1).wait()
            for dy in (1, 3, 2):
                down(s, dy).start()

        @pl.when(jnp.logical_not(is_root))
        def _():
            down(s, 1).wait_recv()

        to_right(s).start()
        to_left(s).start()

    def pass_on(s):
        from_left(s).wait_recv()
        from_right(s).wait_recv()
        forward(s).start()

    def cross(i):
        frm = lax.rem(xy + 16 - i, 16)
        return remote(near_in.at[frm, 1], twin_in.at[frm], fw_s.at[i], fw_r.at[i], twin)

    def cross_step(i, carry):
        plane_in(i).wait_recv()
        cross(i).start()
        return carry

    spread_out(0)
    aa[h, half, :] = activation(1)
    for cp in a_out:
        cp.start()
    relay(0).start()
    spread_out(1)
    pass_on(0)
    own_cross.start()
    lax.fori_loop(1, 16, cross_step, 0)
    spread_out(2)
    for d in (1, 3):
        a_in(d).wait_recv()
        relay(d).start()
    pass_on(1)
    a_in(2).wait_recv()
    relay(2).start()
    spread_out(3)
    pass_on(2)
    for d in range(4):
        relay_in(d).wait_recv()
    from_far(0).wait_recv()
    correlate(0)
    from_far(1).wait_recv()
    correlate(1)
    pass_on(3)
    from_far(2).wait_recv()
    correlate(2)

    own_rows.wait()

    def arrived(i, carry):
        cross(i).wait_recv()
        return carry

    own_cross.wait_recv()
    lax.fori_loop(1, 16, arrived, 0)
    for cp in loads_a:
        cp.wait()
    weight = column[0:UNITS, 1:2]
    outs = []
    for i, out in enumerate((merged_gate, merged_up)):
        got = jnp.dot(
            take_hot[:, : 16 * SLOTS],
            near_in[:, 0, i].reshape(16 * SLOTS, WIDTH),
            preferred_element_type=F32,
        ) + jnp.dot(
            take_hot[:, 16 * SLOTS :],
            twin_in[:, i].reshape(16 * SLOTS, WIDTH),
            preferred_element_type=F32,
        )
        mg_v[i] = ((1.0 - weight) * wa[i].astype(F32) + weight * got).astype(BF16)
        outs.append(pltpu.make_async_copy(mg_v.at[i], out, o_sem.at[i]))
        outs[-1].start()

    from_far(3).wait_recv()
    correlate(3)
    outs.append(pltpu.make_async_copy(corr_v, corr, o_sem.at[2]))
    outs[-1].start()

    for cp in swaps + [to_twin, own_cross] + a_out:
        cp.wait_send()
    for k in range(2):
        for i in range(6):
            ring(k, i).wait_send()

    @pl.when(jnp.logical_not(is_self))
    def _():
        to_root.wait_send()

    for s in range(4):

        @pl.when(is_root)
        def _():
            for dy in (1, 3, 2):
                down(s, dy).wait_send()

        to_right(s).wait_send()
        to_left(s).wait_send()
        forward(s).wait_send()
        relay(s).wait_send()

    def left_all(i, carry):
        plane(i).wait_send()
        cross(i).wait_send()
        return carry

    lax.fori_loop(1, 16, left_all, 0)
    for cp in outs:
        cp.wait()


def body(tokens, gate_a, up_a, gate_b, up_b, matching, mixing):
    any_space = pl.BlockSpec(memory_space=pl.ANY)
    vmem = pl.BlockSpec(memory_space=pltpu.VMEM)
    dma = pltpu.SemaphoreType.DMA
    return pl.pallas_call(
        kernel,
        name="match_merge",
        out_shape=(
            jax.ShapeDtypeStruct((UNITS, 4 * UNITS), BF16),
            jax.ShapeDtypeStruct((UNITS, WIDTH), BF16),
            jax.ShapeDtypeStruct((UNITS, WIDTH), BF16),
        ),
        in_specs=[any_space] * 5 + [vmem] * 2,
        out_specs=(any_space,) * 3,
        scratch_shapes=[
            pltpu.VMEM((2, 1024, WIDTH), BF16),
            pltpu.VMEM((2, 4 * HALF, WIDTH), BF16),
            pltpu.VMEM((2, UNITS, WIDTH), BF16),
            pltpu.VMEM((2, UNITS, WIDTH), BF16),
            pltpu.VMEM((16, 2, 2, SLOTS, WIDTH), BF16),
            pltpu.VMEM((16, 2, 2, SLOTS, WIDTH), BF16),
            pltpu.VMEM((16, 2, SLOTS, WIDTH), BF16),
            pltpu.VMEM((2, 6, HALF, QUARTER), BF16),
            pltpu.VMEM((2, 6, HALF, QUARTER), BF16),
            pltpu.VMEM((2, 4, HALF, QUARTER), F32),
            pltpu.VMEM((HALF, QUARTER), BF16),
            pltpu.VMEM((4, UNITS, QUARTER), BF16),
            pltpu.VMEM((4, 4 * UNITS, QUARTER), BF16),
            pltpu.VMEM((UNITS, 4 * UNITS), F32),
            pltpu.VMEM((UNITS, 4 * UNITS), BF16),
            pltpu.VMEM((2, UNITS, WIDTH), BF16),
            pltpu.VMEM((32 * SLOTS, UNITS), BF16),
            pltpu.VMEM((UNITS, 32 * SLOTS), BF16),
            pltpu.VMEM((8, 512), F32),
            pltpu.VMEM((512, 8), F32),
            dma((10,)),
            dma((8,)),
            dma((8,)),
            dma((16,)),
            dma((16,)),
            dma((16,)),
            dma((16,)),
            dma((2, 6)),
            dma((2, 6)),
            dma((2,)),
            dma((8,)),
            dma((4, 3)),
            dma((4,)),
            dma((4, 3)),
            dma((4, 3)),
            dma((4,)),
            dma((4,)),
            dma((4,)),
            dma((4,)),
            dma((3,)),
        ],
        compiler_params=pltpu.CompilerParams(
            collective_id=0, has_side_effects=True, vmem_limit_bytes=56 * 2**20
        ),
        cost_estimate=pl.CostEstimate(
            flops=8_000_000_000, bytes_accessed=20_000_000, transcendentals=500_000
        ),
    )(tokens, gate_a, up_a, gate_b, up_b, matching.reshape(32, UNITS), mixing.reshape(1, UNITS))


def solution(mesh):
    placed = (
        P(None, "tok"),
        P("fsdp", "tok"),
        P("fsdp", "tok"),
        P("fsdp", "tok"),
        P("fsdp", "tok"),
        P(),
        P("fsdp"),
    )
    return jax.shard_map(
        body,
        mesh=mesh,
        in_specs=placed,
        out_specs=(P("fsdp", "tok"), P("fsdp", "tok"), P("fsdp", "tok")),
        check_vma=False,
    )
```

time: 139 us -> 100 us (0.72)
  Pallas kernels: 123 us -> 91.9 us
  other arithmetic: 6.59 us -> 0 us
  local copies, waits for them, and re-layouts: 8.45 us -> 6.72 us
    pallas_call x1, Pallas kernels: 123 us -> 91.9 us  [body(): pl.pallas_call(kernel, name='match_merge', out_shape=(jax.ShapeDtypeStruc...]
    another operation x7 -> x0, other arithmetic: 2.59 us -> none
    unnamed x9 -> x7, local copies, waits for them, and re-layouts: 5.2 us -> 5.19 us
where the time goes in v2:
time: 100 us; the launch traced here: 99.3 us
  Pallas kernels  91.9 us (92%)
  local copies, waits for them, and re-layouts  6.72 us (7%)
    pallas_call x1, Pallas kernels, body(): pl.pallas_call(kernel, name='match_merge', out_shape=(jax.ShapeDtypeStruc...  91.9 us
    unnamed x7, local copies, waits for them, and re-layouts  5.19 us

profile of v2, /device:TPU:56, one launch (start us, length us, event | category | flops | bytes accessed | tf_op | source)
XLA Modules:
  0.0 99.3 jit_solution(12092392691739380887)
XLA Ops:
  0.6 1.5 %reshape.12.table = s32[32,448]{1,0:T(8,128)} reshape(s32[14336]{0:T(1024)} %param.12) | data formatting | bytes 114688 | tf_op jit(solution)/shard_map/reshape | solution.py:525
  2.2 91.9 %match_merge.1 = (bf16[448,1792]{1,0:T(8,128)(2,1)}, bf16[448,1024]{1,0:T(8,128)(2,1)}, bf16[448,1024]{1,0:T(8,128)(2,1)}) custom-call(bf16[1024,1024]{1,0:T(8,128)(2,1)} %tok.1, bf16[448,1024]{1,0:T(8,128)(2,1)} %gate_a.1, bf16[448,1024]{1,0:T(8,128)(2,1)} %up_a.1, bf16[448,1024]{1,0:T(8,128)(2,1)} %gate_b.1, bf16[448,1024]{1,0:T(8,128)(2,1)} %up_b.1, ...), custom_call_target="tpu_custom_call" | custom-call | flops 8000000000 | bytes 20000000 | tf_op jit(solution)/shard_map/match_merge/pallas_call | solution.py:467
  94.1 0.0 copy-start.1
  94.1 2.8 %copy.13 = bf16[448,1792]{1,0:T(8,128)(2,1)} copy(bf16[448,1792]{1,0:T(8,128)(2,1)} %get-tuple-element.6) | data formatting | bytes 3211264
  96.8 0.0 copy-done.1
  96.9 0.0 copy-start
  96.9 0.9 copy.14
  97.8 0.6 copy-done
  98.4 0.9 copy.15
Async XLA Ops:
  94.1 2.8 %copy-start.1 = (bf16[448,1024]{1,0:T(8,128)(2,1)S(1)}, bf16[448,1024]{1,0:T(8,128)(2,1)}, u32[]{:S(2)}) copy-start(bf16[448,1024]{1,0:T(8,128)(2,1)} %get-tuple-element.7) | copy-start | bytes 2752516
  96.9 1.5 %copy-start = (bf16[448,1024]{1,0:T(8,128)(2,1)S(1)}, bf16[448,1024]{1,0:T(8,128)(2,1)}, u32[]{:S(2)}) copy-start(bf16[448,1024]{1,0:T(8,128)(2,1)} %get-tuple-element.8) | copy-start | bytes 2752516

commit v3 on v2

--- a/solution.py
+++ b/solution.py
@@ -33,7 +33,7 @@
     tok, gate_a, up_a, gate_b, up_b, table, mixing,
     corr, merged_gate, merged_up,
     tk, wh, wb, wa, outb, near_in, twin_in, sb, rb, keep, ab, aa, bb, acc, corr_v, mg_v,
-    send_hot, take_hot, line, column,
+    send_hot, take_hot, line, column, blocks,
     l_sem, xs_s, xs_r, as_s, as_r, fw_s, fw_r, rs_s, rs_r, b1_s, b1_r, b2_s, b2_r, b3_s, b3_r,
     az_s, az_r, ac_s, ac_r, o_sem,
 ):
@@ -83,12 +83,15 @@
     for cp in loads_b + loads[:2] + [load_tok] + loads[2:] + loads_a:
         cp.start()
 
+    strips = [table[pl.ds(i, 16, stride=7), :] for i in range(7)]
+    blocks[0:16, :] = jnp.concatenate(strips[0:4], axis=1)[:, :UNITS]
+    blocks[16:32, :] = jnp.concatenate(strips[3:7], axis=1)[:, 4 * 128 - UNITS :]
     low = f * UNITS
-    value = table[...]
+    value = blocks[...]
     local = value - low
     chosen = jnp.logical_and(local >= 0, local < UNITS)
     source = lax.broadcasted_iota(jnp.int32, (32, UNITS), 0)
-    wanted = table[pl.ds(f, 1), :] - source * UNITS
+    wanted = blocks[pl.ds(lax.div(f, 2) + 16 * lax.rem(f, 2), 1), :] - source * UNITS
     same = jnp.logical_and(wanted >= 0, wanted < UNITS)
     before = (
         lax.broadcasted_iota(jnp.int32, (UNITS, UNITS), 0)
@@ -107,7 +110,9 @@
         == column[0:UNITS, 0:1].astype(jnp.int32)
     ).astype(F32).astype(BF16)
     slot_row = lax.broadcasted_iota(jnp.int32, (32 * SLOTS, 32), 0)
-    to_block = lax.rem(lax.broadcasted_iota(jnp.int32, (32 * SLOTS, 32), 1) + 16 * l, 32)
+    held = lax.broadcasted_iota(jnp.int32, (32 * SLOTS, 32), 1)
+    held = 2 * jnp.bitwise_and(held, 15) + lax.shift_right_logical(held, 4)
+    to_block = lax.rem(held + 16 * l, 32)
     spread = (lax.shift_right_logical(slot_row, 4) == to_block).astype(F32).astype(BF16)
 
     def widen(v):
@@ -495,6 +500,7 @@
             pltpu.VMEM((UNITS, 32 * SLOTS), BF16),
             pltpu.VMEM((8, 512), F32),
             pltpu.VMEM((512, 8), F32),
+            pltpu.VMEM((32, UNITS), jnp.int32),
             dma((10,)),
             dma((8,)),
             dma((8,)),
@@ -522,7 +528,7 @@
         cost_estimate=pl.CostEstimate(
             flops=8_000_000_000, bytes_accessed=20_000_000, transcendentals=500_000
         ),
-    )(tokens, gate_a, up_a, gate_b, up_b, matching.reshape(32, UNITS), mixing.reshape(1, UNITS))
+    )(tokens, gate_a, up_a, gate_b, up_b, matching.reshape(112, 128), mixing.reshape(1, UNITS))
 
 
 def solution(mesh):

time: 100 us -> 99.1 us (level)
  local copies, waits for them, and re-layouts: 6.72 us -> 5.19 us
    reshape x1 -> x0, local copies, waits for them, and re-layouts: 1.53 us -> none  [body(): matching.reshape(32, UNITS)]
where the time goes in v3:
time: 99.1 us; the launch traced here: 98.1 us
  Pallas kernels  92.3 us (93%)
  local copies, waits for them, and re-layouts  5.19 us (5%)
    pallas_call x1, Pallas kernels, body(): pl.pallas_call(kernel, name='match_merge', out_shape=(jax.ShapeDtypeStruc...  92.3 us
    unnamed x7, local copies, waits for them, and re-layouts  5.19 us

profile of v3, /device:TPU:56, one launch (start us, length us, event | category | flops | bytes accessed | tf_op | source)
XLA Modules:
  0.0 98.1 jit_solution(15407660204584379088)
XLA Ops:
  0.6 92.3 %match_merge.1 = (bf16[448,1792]{1,0:T(8,128)(2,1)}, bf16[448,1024]{1,0:T(8,128)(2,1)}, bf16[448,1024]{1,0:T(8,128)(2,1)}) custom-call(bf16[1024,1024]{1,0:T(8,128)(2,1)} %tok.1, bf16[448,1024]{1,0:T(8,128)(2,1)} %gate_a.1, bf16[448,1024]{1,0:T(8,128)(2,1)} %up_a.1, bf16[448,1024]{1,0:T(8,128)(2,1)} %gate_b.1, bf16[448,1024]{1,0:T(8,128)(2,1)} %up_b.1, ...), custom_call_target="tpu_custom_call" | custom-call | flops 8000000000 | bytes 20000000 | tf_op jit(solution)/shard_map/match_merge/pallas_call | solution.py:472
  92.9 0.0 copy-start.1
  92.9 2.8 %copy.13 = bf16[448,1792]{1,0:T(8,128)(2,1)} copy(bf16[448,1792]{1,0:T(8,128)(2,1)} %get-tuple-element.6) | data formatting | bytes 3211264
  95.7 0.0 copy-done.1
  95.7 0.0 copy-start
  95.7 0.9 copy.14
  96.6 0.6 copy-done
  97.2 0.9 copy.15
Async XLA Ops:
  92.9 2.8 %copy-start.1 = (bf16[448,1024]{1,0:T(8,128)(2,1)S(1)}, bf16[448,1024]{1,0:T(8,128)(2,1)}, u32[]{:S(2)}) copy-start(bf16[448,1024]{1,0:T(8,128)(2,1)} %get-tuple-element.7) | copy-start | bytes 2752516
  95.7 1.5 %copy-start = (bf16[448,1024]{1,0:T(8,128)(2,1)S(1)}, bf16[448,1024]{1,0:T(8,128)(2,1)}, u32[]{:S(2)}) copy-start(bf16[448,1024]{1,0:T(8,128)(2,1)} %get-tuple-element.8) | copy-start | bytes 2752516
